TPU v7x, 32 devices: a whole 2x2x4 slice. The times are simulated.
32 devices in a mesh: table: 16 (over z, y, x), score: 2 (over core).
Axes of the slice: x: 2, y: 2, z: 4, core: 2. Of those that a mesh axis runs over, the one named last changes fastest.
Arguments:
- hot_item_table: float32 [2048, 128], replicated, may hold values from -6 to 6
- cold_item_table: float32 [16384, 128], P('table'), may hold values from -6 to 6
- hist_rows: int32 [128, 512], P('table', 'score'), may hold values from 0 to 18431, as said below
- cand_rows: int32 [128, 512], P('table', 'score'), may hold values from 0 to 18431, as said below
- w_query: bfloat16 [128, 128], replicated, may hold values from -0.5 to 0.5
- w_key: bfloat16 [128, 128], replicated, may hold values from -0.5 to 0.5
- w_first: bfloat16 [256, 1024], replicated, may hold values from -0.5 to 0.5
- w_second: bfloat16 [1, 1024, 1024], replicated, may hold values from -0.25 to 0.25
- w_out: bfloat16 [1024], replicated, may hold values from -0.25 to 0.25
Outputs:
- scores: float32 [128, 512], P('table', 'score')
Inputs may be any that keep to these rules, and one draw needn't show every extreme that they name: `hist_rows`: among the history items of one device (8 requests, 256 items each), at most 128 name cold rows of any one owner; for each index along score, one owner is named exactly 128 times by every device along table. `cand_rows`: among the candidates of one device (8 requests, 256 candidates each), at most 128 name cold rows of any one owner; for each index along score, one owner is named exactly 128 times by every device along table.
All inputs are finite; a program needn't handle non-finite values.
Results may differ from a plain program's by a relative error of at most 0.0072.
Values may be sent and summed in bfloat16 or wider, within the bound.
A program may use at most 64 MiB of HBM per device.

v0:
```python
import math

import jax
import jax.numpy as jnp
from jax import lax
from jax.sharding import PartitionSpec as P

H = 512
HOT = 2048
COLD_DEV = 1024


def owner_positions(owner_match):
    item_total, owner_count = owner_match.shape
    block = math.gcd(item_total, 128)
    blocks = item_total // block
    match_bf = owner_match.astype(jnp.bfloat16).reshape(blocks, block, owner_count)
    lower = (
        lax.broadcasted_iota(jnp.int32, (block, block), 0)
        > lax.broadcasted_iota(jnp.int32, (block, block), 1)
    ).astype(jnp.bfloat16)
    within = jnp.einsum("ij,kjo->kio", lower, match_bf, preferred_element_type=jnp.float32)
    totals = jnp.sum(match_bf.astype(jnp.float32), axis=1)
    offsets = jnp.cumsum(totals, axis=0) - totals
    before = (within + offsets[:, None, :]).reshape(item_total, owner_count)
    return jnp.sum(before * owner_match, axis=1).astype(jnp.int32)


def gather_owner_rows(
    grouped_item_codes, owner_capacity_list, hot_item_table, cold_item_table, table_row_count
):
    owner_iota = jnp.arange(table_row_count, dtype=jnp.int32)
    layouts = []
    outgoing = []
    for item_row_codes, slot_capacity in zip(grouped_item_codes, owner_capacity_list):
        is_cold = item_row_codes >= HOT
        relative = jnp.where(is_cold, item_row_codes - HOT, 0)
        owner_id = relative // COLD_DEV
        slot_id = relative % COLD_DEV
        owner_match = jnp.logical_and(
            owner_id[:, None] == owner_iota[None, :], is_cold[:, None]
        ).astype(jnp.float32)
        position = owner_positions(owner_match)
        flat_index = owner_id * slot_capacity + position
        slot_onehot = (
            position[:, None] == jnp.arange(slot_capacity, dtype=jnp.int32)[None, :]
        ).astype(jnp.float32)
        weighted = owner_match * slot_id.astype(jnp.float32)[:, None]
        requests_out = jnp.einsum(
            "io,is->os",
            weighted,
            slot_onehot,
            precision=lax.Precision.HIGHEST,
            preferred_element_type=jnp.float32,
        )
        outgoing.append(requests_out.astype(jnp.int32))
        layouts.append((item_row_codes, is_cold, flat_index, slot_capacity))
    wanted_all = jnp.concatenate(outgoing, axis=1)
    cold_rows = jnp.take(
        cold_item_table,
        lax.all_to_all(wanted_all, "table", split_axis=0, concat_axis=0, tiled=True),
        axis=0,
    ).astype(jnp.bfloat16)
    fetched = lax.all_to_all(cold_rows, "table", split_axis=0, concat_axis=0, tiled=True)
    results = []
    column_start = 0
    for item_row_codes, is_cold, flat_index, slot_capacity in layouts:
        flat_rows = fetched[:, column_start : column_start + slot_capacity].reshape(
            table_row_count * slot_capacity, fetched.shape[2]
        )
        picked = jnp.take(flat_rows, jnp.where(is_cold, flat_index, 0), axis=0)
        hot_rows = jnp.take(hot_item_table, jnp.where(is_cold, 0, item_row_codes), axis=0).astype(
            jnp.bfloat16
        )
        results.append(jnp.where(is_cold[:, None], picked, hot_rows))
        column_start = column_start + slot_capacity
    return results


def body(
    hot_item_table, cold_item_table, hist_rows, cand_rows, w_query, w_key, w_first, w_second, w_out
):
    table_row_count = lax.axis_size("table")
    requests, h_dev = hist_rows.shape
    c_dev = cand_rows.shape[1]
    width = hot_item_table.shape[1]
    cap_h = max(2, requests * h_dev // table_row_count)
    cap_c = max(2, requests * c_dev // table_row_count)
    history_emb, candidate_emb = gather_owner_rows(
        [hist_rows.reshape(-1), cand_rows.reshape(-1)],
        [cap_h, cap_c],
        hot_item_table,
        cold_item_table,
        table_row_count,
    )
    candidate_bf = candidate_emb.reshape(requests, c_dev, width)
    queries = jnp.einsum(
        "rce,ea->rca", candidate_bf, w_query, preferred_element_type=jnp.float32
    ).astype(jnp.bfloat16)
    score_scale = 1.0 / math.sqrt(w_query.shape[1])
    history_bf = history_emb.reshape(requests, h_dev, width)
    shard_rows = lax.all_gather(history_bf, "score", axis=1, tiled=True)
    key_rows = jnp.einsum(
        "rhe,ea->rha", shard_rows, w_key, preferred_element_type=jnp.float32
    ).astype(jnp.bfloat16)
    logits = (
        jnp.einsum("rca,rha->rch", queries, key_rows, preferred_element_type=jnp.float32)
        * score_scale
    )
    weights = jax.nn.sigmoid(logits).astype(jnp.bfloat16)
    pooled_sum = jnp.einsum("rch,rhe->rce", weights, shard_rows, preferred_element_type=jnp.float32)
    pooled = (pooled_sum * (1.0 / math.sqrt(H))).astype(jnp.bfloat16)
    joined = jnp.concatenate([candidate_bf, pooled], axis=2).reshape(requests * c_dev, 2 * width)
    hidden = jnp.maximum(jnp.dot(joined, w_first, preferred_element_type=jnp.float32), 0.0).astype(
        jnp.bfloat16
    )
    hidden = jnp.maximum(
        jnp.dot(hidden, w_second[0], preferred_element_type=jnp.float32), 0.0
    ).astype(jnp.bfloat16)
    ranked = jnp.dot(hidden, w_out, preferred_element_type=jnp.float32)
    return ranked.reshape(requests, c_dev)


def solution(mesh):
    return jax.shard_map(
        body,
        mesh=mesh,
        in_specs=(
            P(),
            P("table", None),
            P("table", "score"),
            P("table", "score"),
            P(),
            P(),
            P(),
            P(),
            P(),
        ),
        out_specs=P("table", "score"),
        check_vma=False,
    )
```

profile of v0, /device:TPU:0, one launch (start us, length us, event | category | flops | bytes accessed | tf_op | source)
XLA Modules:
  0.0 134.1 jit_solution(995421544298405222)
XLA Ops:
  6.5 0.9 broadcast_compare_fusion.1
  7.4 0.7 broadcast_add_fusion.1
  8.1 0.7 broadcast_compare_fusion
  9.9 0.7 copy.13
  11.0 0.7 copy.12
  11.8 2.1 %convolution_convert_fusion.3 = s32[16,128]{1,0:T(8,128)S(1)} fusion(s32[2048]{0:T(1024)S(1)} %convert_bitcast_fusion.1, f32[2048]{0:T(1024)S(1)} %get-tuple-element.16, s32[2048]{0:T(1024)S(1)} %get-tuple-element.8, pred[2048]{0:T(1024)(128)(4,1)S(1)} %get-tuple-element.9), kind=kOutput, calls=%fused_computation.23 | convolution fusion | flops 50694144 | bytes 34816 | tf_op jit(solution)/shard_map/io,is->os/dot_general | solution.py:49
  13.9 2.1 %convolution_convert_fusion.2 = s32[16,128]{1,0:T(8,128)S(1)} fusion(s32[2048]{0:T(1024)S(1)} %convert_bitcast_fusion, f32[2048]{0:T(1024)S(1)} %get-tuple-element.17, s32[2048]{0:T(1024)S(1)} %get-tuple-element.11, pred[2048]{0:T(1024)(128)(4,1)S(1)} %get-tuple-element.12), kind=kOutput, calls=%fused_computation.22 | convolution fusion | flops 50694144 | bytes 34816 | tf_op jit(solution)/shard_map/io,is->os/dot_general | solution.py:49
  16.1 15.4 %all_to_all.20 = s32[16,1,256]{2,1,0:T(1,128)S(1)} all-to-all(s32[16,1,256]{2,1,0:T(1,128)S(1)} %copy.10), channel_id=1, replica_groups=mesh['table'=16,'score'=2] {'table'}, dimensions={0} | all-to-all | bytes 32768 | tf_op jit(solution)/shard_map/all_to_all | solution.py:61
  31.6 14.2 %gather_fusion = bf16[4096,128]{1,0:T(8,128)(2,1)} fusion(f32[1024,128]{1,0:T(8,128)S(1)} %copy-done.1, s32[4096]{0:T(1024)S(1)} %broadcast_clamp_fusion), kind=kCustom, calls=%fused_computation.4 | custom fusion | bytes 2113536 | tf_op jit(solution)/shard_map/jit(_take)/gather | solution.py:59
  45.8 2.6 %select_convert_fusion = bf16[16,256,128]{2,1,0:T(8,128)(2,1)} fusion(bf16[16,256,128]{2,1,0:T(8,128)(2,1)} %bitcast.68, pred[16,256]{1,0:T(8,128)(4,1)S(1)} %compare_and_fusion), kind=kLoop, calls=%fused_computation.9 | loop fusion | flops 524288 | bytes 2101248 | tf_op jit(solution)/shard_map/convert_element_type | solution.py:63
  48.4 4.3 %all-to-all-start.1 = ((bf16[16,256,128]{2,1,0:T(8,128)(2,1)}), bf16[16,256,128]{2,1,0:T(8,128)(2,1)}, u32[]{:S(2)}, u32[]{:S(2)}) async-start(bf16[16,256,128]{2,1,0:T(8,128)(2,1)} %select_convert_fusion), calls=%async_computation.1 | async-start | bytes 2097152 | tf_op jit(solution)/shard_map/all_to_all | solution.py:64
  53.0 7.6 %gather_fusion.4 = bf16[2048,128]{1,0:T(8,128)(2,1)} fusion(f32[2048,128]{1,0:T(8,128)S(1)} %copy-done.2, s32[2048]{0:T(1024)S(1)} %get-tuple-element.15), kind=kCustom, calls=%fused_computation.3.clone | custom fusion | bytes 1056768 | tf_op jit(solution)/shard_map/jit(_take)/gather | solution.py:72
  60.6 15.4 %all-to-all-done.1 = bf16[16,256,128]{2,1,0:T(8,128)(2,1)} async-done(((bf16[16,256,128]{2,1,0:T(8,128)(2,1)}), bf16[16,256,128]{2,1,0:T(8,128)(2,1)}, u32[]{:S(2)}, u32[]{:S(2)}) %all-to-all-start.1) | async-done | bytes 1048608 | tf_op jit(solution)/shard_map/all_to_all | solution.py:64
  76.1 2.3 %fusion.59 = (bf16[16,128,128]{2,1,0:T(8,128)(2,1)}, bf16[16,128,128]{2,1,0:T(8,128)(2,1)}) fusion(bf16[16,256,128]{2,1,0:T(8,128)(2,1)} %all-to-all-done.1), kind=kLoop, calls=%fused_computation.128 | loop fusion | bytes 2097152 | tf_op jit(solution)/shard_map/slice | solution.py:68
  78.4 8.7 %gather_fusion.3 = bf16[2048,128]{1,0:T(8,128)(2,1)} fusion(bf16[2048,128]{1,0:T(8,128)(2,1)} %bitcast.67, s32[2048]{0:T(1024)S(1)} %get-tuple-element.19), kind=kCustom, calls=%fused_computation.2.clone | custom fusion | bytes 1056768 | tf_op jit(solution)/shard_map/jit(_take)/gather | solution.py:71
  87.1 4.0 %fusion.21 = bf16[2048,128]{1,0:T(8,128)(2,1)} fusion(bf16[2048,128]{1,0:T(8,128)(2,1)} %gather_fusion.4, bf16[2048,128]{1,0:T(8,128)(2,1)} %gather_fusion.3, pred[2048]{0:T(1024)(128)(4,1)S(1)} %compare_and_fusion.1, pred[2048]{0:T(1024)(128)(4,1)S(1)} %get-tuple-element.6, pred[2048]{0:T(1024)(128)(4,1)S(1)} %get-tuple-element.9), kind=kLoop, calls=%fused_computation.38 | loop fusion | flops 786432 | bytes 1579008 | tf_op jit(solution)/shard_map/jit(_where)/select_n | solution.py:75
  91.2 7.6 %gather_fusion.2 = bf16[2048,128]{1,0:T(8,128)(2,1)} fusion(f32[2048,128]{1,0:T(8,128)S(1)} %copy-done.2, s32[2048]{0:T(1024)S(1)} %get-tuple-element.18), kind=kCustom, calls=%fused_computation.1.clone | custom fusion | bytes 1056768 | tf_op jit(solution)/shard_map/jit(_take)/gather | solution.py:72
  98.9 6.9 %gather_fusion.1 = bf16[2048,128]{1,0:T(8,128)(2,1)S(1)} fusion(bf16[2048,128]{1,0:T(8,128)(2,1)} %bitcast.66, s32[2048]{0:T(1024)S(1)} %get-tuple-element.20), kind=kCustom, calls=%fused_computation.clone | custom fusion | bytes 1056768 | tf_op jit(solution)/shard_map/jit(_take)/gather | solution.py:71
  105.8 1.6 %fusion.20 = bf16[2048,128]{1,0:T(8,128)(2,1)S(1)} fusion(bf16[2048,128]{1,0:T(8,128)(2,1)S(1)} %copy-done.3, bf16[2048,128]{1,0:T(8,128)(2,1)S(1)} %gather_fusion.1, pred[2048]{0:T(1024)(128)(4,1)S(1)} %compare_and_fusion.3, pred[2048]{0:T(1024)(128)(4,1)S(1)} %get-tuple-element.10, pred[2048]{0:T(1024)(128)(4,1)S(1)} %get-tuple-element.12), kind=kLoop, calls=%fused_computation.37 | loop fusion | flops 786432 | bytes 1579008 | tf_op jit(solution)/shard_map/jit(_where)/select_n | solution.py:75
  107.4 0.8 copy-done.4
  108.6 4.0 %divide_convert_fusion = bf16[8,256,512]{2,1,0:T(8,128)(2,1)} fusion(bf16[8,256,128]{2,1,0:T(8,128)(2,1)S(1)} %convolution_convert_fusion.1, bf16[8,512,128]{2,1,0:T(8,128)(2,1)} %all-gather.2.cloned.1.call-done, bf16[128,128]{1,0:T(8,128)(2,1)S(1)} %copy-done.8), kind=kOutput, calls=%fused_computation.7 | convolution fusion | flops 408420352 | bytes 3702784 | tf_op jit(solution)/shard_map/rca,rha->rch/dot_general | solution.py:107
  112.6 2.5 %fusion.1 = bf16[8,256,128]{2,1,0:T(8,128)(2,1)S(1)} fusion(bf16[8,256,512]{2,1,0:T(8,128)(2,1)} %divide_convert_fusion, bf16[8,512,128]{2,1,0:T(8,128)(2,1)} %all-gather.2.cloned.1.call-done), kind=kOutput, calls=%fused_computation.13 | convolution fusion | flops 268959744 | bytes 3670016 | tf_op jit(solution)/shard_map/rch,rhe->rce/dot_general | solution.py:111
  115.2 8.1 %maximum_convert_fusion = bf16[2048,1024]{1,0:T(8,128)(2,1)} fusion(bf16[1,1024,1024]{2,1,0:T(8,128)(2,1)S(1)} %copy-done, bf16[256,1024]{1,0:T(8,128)(2,1)} %param.19, bf16[2048,128]{1,0:T(8,128)(2,1)S(1)} %bitcast.81, bf16[2048,128]{1,0:T(8,128)(2,1)S(1)} %copy-done.5), kind=kOutput, calls=%fused_computation.5 | convolution fusion | flops 5379194880 | bytes 7864320 | tf_op jit(solution)/shard_map/dot_general | solution.py:118
  123.3 3.4 %fusion.60 = f32[1,2048]{1,0:T(1,128)S(1)} fusion(bf16[2048,1024]{1,0:T(8,128)(2,1)} %maximum_convert_fusion, bf16[1024,1]{0,1:T(2,128)(2,1)S(1)} %reshape.328), kind=kOutput, calls=%fused_computation.129 | convolution fusion | flops 4194304 | bytes 4204544 | tf_op jit(solution)/shard_map/dot_general | solution.py:120
  (51 shorter events, 2.8 us)
Async XLA Ops:
  6.5 108.6 %copy-start = (bf16[1,1024,1024]{2,1,0:T(8,128)(2,1)S(1)}, bf16[1,1024,1024]{2,1,0:T(8,128)(2,1)}, u32[]{:S(2)}) copy-start(bf16[1,1024,1024]{2,1,0:T(8,128)(2,1)} %param.20) | copy-start | bytes 6291460
  6.5 25.0 %copy-start.1 = (f32[1024,128]{1,0:T(8,128)S(1)}, f32[1024,128]{1,0:T(8,128)}, u32[]{:S(2)}) copy-start(f32[1024,128]{1,0:T(8,128)} %param.14) | copy-start | bytes 1572868
  45.8 7.2 %copy-start.2 = (f32[2048,128]{1,0:T(8,128)S(1)}, f32[2048,128]{1,0:T(8,128)}, u32[]{:S(2)}) copy-start(f32[2048,128]{1,0:T(8,128)} %param.13) | copy-start | bytes 3145732
  48.4 27.6 %all-to-all-start.1 = ((bf16[16,256,128]{2,1,0:T(8,128)(2,1)}), bf16[16,256,128]{2,1,0:T(8,128)(2,1)}, u32[]{:S(2)}, u32[]{:S(2)}) async-start(bf16[16,256,128]{2,1,0:T(8,128)(2,1)} %select_convert_fusion), calls=%async_computation.1 | async-start | bytes 2097152 | tf_op jit(solution)/shard_map/all_to_all | solution.py:64
  52.8 55.8 %all-gather.2.cloned.1.call-start = ((), (), s32[]{:S(2)}) async-start(), calls=%async_computation.2 | async-start | bytes 1572864 | tf_op jit(solution)/shard_map/all_gather | solution.py:102
  87.1 11.7 %copy-start.7 = (bf16[1024]{0:T(1024)(128)(2,1)S(1)}, bf16[1024]{0:T(1024)(128)(2,1)}, u32[]{:S(2)}) copy-start(bf16[1024]{0:T(1024)(128)(2,1)} %param.21) | copy-start | bytes 6148
  98.8 6.9 %copy-start.3 = (bf16[2048,128]{1,0:T(8,128)(2,1)S(1)}, bf16[2048,128]{1,0:T(8,128)(2,1)}, u32[]{:S(2)}) copy-start(bf16[2048,128]{1,0:T(8,128)(2,1)} %gather_fusion.2) | copy-start | bytes 1572868
  98.8 9.4 %copy-start.6 = (bf16[128,128]{1,0:T(8,128)(2,1)S(1)}, bf16[128,128]{1,0:T(8,128)(2,1)}, u32[]{:S(2)}) copy-start(bf16[128,128]{1,0:T(8,128)(2,1)} %param.17) | copy-start | bytes 98308
  98.8 9.7 %copy-start.8 = (bf16[128,128]{1,0:T(8,128)(2,1)S(1)}, bf16[128,128]{1,0:T(8,128)(2,1)}, u32[]{:S(2)}) copy-start(bf16[128,128]{1,0:T(8,128)(2,1)} %param.18) | copy-start | bytes 98308
  107.4 0.8 copy-start.4
  108.5 6.7 %copy-start.5 = (bf16[2048,128]{1,0:T(8,128)(2,1)S(1)}, bf16[2048,128]{1,0:T(8,128)(2,1)}, u32[]{:S(2)}) copy-start(bf16[2048,128]{1,0:T(8,128)(2,1)} %copy-done.4) | copy-start | bytes 1572868
Sparse Core Ops, SparseCore 0:
  91.3 9.2 all-gather.1
where the time goes:
time: 135 us; the launch traced here: 134 us
  local copies, waits for them, and re-layouts  50.3 us (37%)
  matrix products  23 us (17%)
  blocking collectives  15.4 us (11%)
  waiting for transfers between devices  15.4 us (11%)
  between operations  13.7 us (10%)
  other arithmetic  11.8 us (9%)
  starting transfers between devices  4.55 us (3%)
    gather x2, local copies, waits for them, and re-layouts, gather_owner_rows(): picked = jnp.take(flat_rows, jnp.where(is_cold, flat_index, 0), axis=0)  15.6 us
    all_to_all x1, blocking collectives, gather_owner_rows(): lax.all_to_all(wanted_all, 'table', split_axis=0, concat_axis=0, tiled=True)  15.4 us
    all_to_all x1, waiting for transfers between devices, gather_owner_rows(): lax.all_to_all(cold_rows, 'table', split_axis=0, concat_axis=0, tiled=True)  15.4 us
    gather x2, local copies, waits for them, and re-layouts, gather_owner_rows(): jnp.take(hot_item_table, jnp.where(is_cold, 0, item_row_codes), axis=0)  15.3 us
    gather x1, local copies, waits for them, and re-layouts, gather_owner_rows(): jnp.take(cold_item_table, lax.all_to_all(wanted_all, 'table', split_axis=...  14.2 us
    dot_general x1, matrix products, body(): jnp.dot(hidden, w_second[0], preferred_element_type=jnp.float32)  8.13 us
    select_n x2, other arithmetic, gather_owner_rows(): results.append(jnp.where(is_cold[:, None], picked, hot_rows))  5.69 us
    all_to_all x1, starting transfers between devices, gather_owner_rows(): lax.all_to_all(cold_rows, 'table', split_axis=0, concat_axis=0, tiled=True)  4.33 us
  transfers between devices with their start and end apart: 2, of which 1 were waited for; matrix products, arithmetic and copies ran while one was open for 18% of the time, Pallas kernels for 0%

commit v1 on v0

--- a/solution.py
+++ b/solution.py
@@ -21,7 +21,13 @@
     ).astype(jnp.bfloat16)
     within = jnp.einsum("ij,kjo->kio", lower, match_bf, preferred_element_type=jnp.float32)
     totals = jnp.sum(match_bf.astype(jnp.float32), axis=1)
-    offsets = jnp.cumsum(totals, axis=0) - totals
+    earlier = (
+        lax.broadcasted_iota(jnp.int32, (blocks, blocks), 0)
+        > lax.broadcasted_iota(jnp.int32, (blocks, blocks), 1)
+    ).astype(jnp.float32)
+    offsets = jnp.einsum(
+        "bk,ko->bo", earlier, totals, precision=lax.Precision.HIGHEST, preferred_element_type=jnp.float32
+    )
     before = (within + offsets[:, None, :]).reshape(item_total, owner_count)
     return jnp.sum(before * owner_match, axis=1).astype(jnp.int32)
 

time: 135 us -> 135 us (level)
  no operation moved by 1% of the time
where the time goes in v1:
time: 135 us; the launch traced here: 134 us
  local copies, waits for them, and re-layouts  50.4 us (37%)
  matrix products  23.2 us (17%)
  waiting for transfers between devices  15.5 us (11%)
  blocking collectives  15.4 us (11%)
  between operations  13.7 us (10%)
  other arithmetic  11.7 us (9%)
  starting transfers between devices  4.56 us (3%)
    gather x2, local copies, waits for them, and re-layouts, gather_owner_rows(): picked = jnp.take(flat_rows, jnp.where(is_cold, flat_index, 0), axis=0)  15.6 us
    all_to_all x1, blocking collectives, gather_owner_rows(): lax.all_to_all(wanted_all, 'table', split_axis=0, concat_axis=0, tiled=True)  15.4 us
    all_to_all x1, waiting for transfers between devices, gather_owner_rows(): lax.all_to_all(cold_rows, 'table', split_axis=0, concat_axis=0, tiled=True)  15.4 us
    gather x2, local copies, waits for them, and re-layouts, gather_owner_rows(): jnp.take(hot_item_table, jnp.where(is_cold, 0, item_row_codes), axis=0)  15.2 us
    gather x1, local copies, waits for them, and re-layouts, gather_owner_rows(): jnp.take(cold_item_table, lax.all_to_all(wanted_all, 'table', split_axis=...  14.2 us
    dot_general x1, matrix products, body(): jnp.dot(hidden, w_second[0], preferred_element_type=jnp.float32)  8.14 us
    select_n x2, other arithmetic, gather_owner_rows(): results.append(jnp.where(is_cold[:, None], picked, hot_rows))  5.69 us
    all_to_all x1, starting transfers between devices, gather_owner_rows(): lax.all_to_all(cold_rows, 'table', split_axis=0, concat_axis=0, tiled=True)  4.34 us
  transfers between devices with their start and end apart: 2, of which 1 were waited for; matrix products, arithmetic and copies ran while one was open for 18% of the time, Pallas kernels for 0%

profile of v1, /device:TPU:0, one launch (start us, length us, event | category | flops | bytes accessed | tf_op | source)
XLA Modules:
  0.0 134.4 jit_solution(15087299233577586099)
XLA Ops:
  6.5 0.9 broadcast_compare_fusion.1
  7.4 0.7 broadcast_add_fusion.1
  8.1 0.7 broadcast_compare_fusion
  10.0 0.7 copy.13
  11.2 0.7 copy.12
  12.0 2.1 %convolution_convert_fusion.3 = s32[16,128]{1,0:T(8,128)S(1)} fusion(s32[2048]{0:T(1024)S(1)} %convert_bitcast_fusion.1, f32[2048]{0:T(1024)S(1)} %get-tuple-element.16, s32[2048]{0:T(1024)S(1)} %get-tuple-element.8, pred[2048]{0:T(1024)(128)(4,1)S(1)} %get-tuple-element.9), kind=kOutput, calls=%fused_computation.23 | convolution fusion | flops 50694144 | bytes 34816 | tf_op jit(solution)/shard_map/io,is->os/dot_general | solution.py:55
  14.1 2.1 %convolution_convert_fusion.2 = s32[16,128]{1,0:T(8,128)S(1)} fusion(s32[2048]{0:T(1024)S(1)} %convert_bitcast_fusion, f32[2048]{0:T(1024)S(1)} %get-tuple-element.17, s32[2048]{0:T(1024)S(1)} %get-tuple-element.11, pred[2048]{0:T(1024)(128)(4,1)S(1)} %get-tuple-element.12), kind=kOutput, calls=%fused_computation.22 | convolution fusion | flops 50694144 | bytes 34816 | tf_op jit(solution)/shard_map/io,is->os/dot_general | solution.py:55
  16.2 15.4 %all_to_all.20 = s32[16,1,256]{2,1,0:T(1,128)S(1)} all-to-all(s32[16,1,256]{2,1,0:T(1,128)S(1)} %copy.10), channel_id=1, replica_groups=mesh['table'=16,'score'=2] {'table'}, dimensions={0} | all-to-all | bytes 32768 | tf_op jit(solution)/shard_map/all_to_all | solution.py:67
  31.7 14.2 %gather_fusion = bf16[4096,128]{1,0:T(8,128)(2,1)} fusion(f32[1024,128]{1,0:T(8,128)S(1)} %copy-done.1, s32[4096]{0:T(1024)S(1)} %broadcast_clamp_fusion), kind=kCustom, calls=%fused_computation.4 | custom fusion | bytes 2113536 | tf_op jit(solution)/shard_map/jit(_take)/gather | solution.py:65
  46.0 2.6 %select_convert_fusion = bf16[16,256,128]{2,1,0:T(8,128)(2,1)} fusion(bf16[16,256,128]{2,1,0:T(8,128)(2,1)} %bitcast.70, pred[16,256]{1,0:T(8,128)(4,1)S(1)} %compare_and_fusion), kind=kLoop, calls=%fused_computation.9 | loop fusion | flops 524288 | bytes 2101248 | tf_op jit(solution)/shard_map/convert_element_type | solution.py:69
  48.6 4.3 %all-to-all-start.1 = ((bf16[16,256,128]{2,1,0:T(8,128)(2,1)}), bf16[16,256,128]{2,1,0:T(8,128)(2,1)}, u32[]{:S(2)}, u32[]{:S(2)}) async-start(bf16[16,256,128]{2,1,0:T(8,128)(2,1)} %select_convert_fusion), calls=%async_computation.1 | async-start | bytes 2097152 | tf_op jit(solution)/shard_map/all_to_all | solution.py:70
  53.2 7.6 %gather_fusion.4 = bf16[2048,128]{1,0:T(8,128)(2,1)} fusion(f32[2048,128]{1,0:T(8,128)S(1)} %copy-done.2, s32[2048]{0:T(1024)S(1)} %get-tuple-element.15), kind=kCustom, calls=%fused_computation.3.clone | custom fusion | bytes 1056768 | tf_op jit(solution)/shard_map/jit(_take)/gather | solution.py:78
  60.8 15.4 %all-to-all-done.1 = bf16[16,256,128]{2,1,0:T(8,128)(2,1)} async-done(((bf16[16,256,128]{2,1,0:T(8,128)(2,1)}), bf16[16,256,128]{2,1,0:T(8,128)(2,1)}, u32[]{:S(2)}, u32[]{:S(2)}) %all-to-all-start.1) | async-done | bytes 1048608 | tf_op jit(solution)/shard_map/all_to_all | solution.py:70
  76.3 2.3 %fusion.61 = (bf16[16,128,128]{2,1,0:T(8,128)(2,1)}, bf16[16,128,128]{2,1,0:T(8,128)(2,1)}) fusion(bf16[16,256,128]{2,1,0:T(8,128)(2,1)} %all-to-all-done.1), kind=kLoop, calls=%fused_computation.131 | loop fusion | bytes 2097152 | tf_op jit(solution)/shard_map/slice | solution.py:74
  78.6 8.8 %gather_fusion.3 = bf16[2048,128]{1,0:T(8,128)(2,1)} fusion(bf16[2048,128]{1,0:T(8,128)(2,1)} %bitcast.69, s32[2048]{0:T(1024)S(1)} %get-tuple-element.19), kind=kCustom, calls=%fused_computation.2.clone | custom fusion | bytes 1056768 | tf_op jit(solution)/shard_map/jit(_take)/gather | solution.py:77
  87.4 4.0 %fusion.21 = bf16[2048,128]{1,0:T(8,128)(2,1)} fusion(bf16[2048,128]{1,0:T(8,128)(2,1)} %gather_fusion.4, bf16[2048,128]{1,0:T(8,128)(2,1)} %gather_fusion.3, pred[2048]{0:T(1024)(128)(4,1)S(1)} %compare_and_fusion.1, pred[2048]{0:T(1024)(128)(4,1)S(1)} %get-tuple-element.6, pred[2048]{0:T(1024)(128)(4,1)S(1)} %get-tuple-element.9), kind=kLoop, calls=%fused_computation.38 | loop fusion | flops 786432 | bytes 1579008 | tf_op jit(solution)/shard_map/jit(_where)/select_n | solution.py:81
  91.4 7.6 %gather_fusion.2 = bf16[2048,128]{1,0:T(8,128)(2,1)} fusion(f32[2048,128]{1,0:T(8,128)S(1)} %copy-done.2, s32[2048]{0:T(1024)S(1)} %get-tuple-element.18), kind=kCustom, calls=%fused_computation.1.clone | custom fusion | bytes 1056768 | tf_op jit(solution)/shard_map/jit(_take)/gather | solution.py:78
  99.1 6.9 %gather_fusion.1 = bf16[2048,128]{1,0:T(8,128)(2,1)S(1)} fusion(bf16[2048,128]{1,0:T(8,128)(2,1)} %bitcast.68, s32[2048]{0:T(1024)S(1)} %get-tuple-element.20), kind=kCustom, calls=%fused_computation.clone | custom fusion | bytes 1056768 | tf_op jit(solution)/shard_map/jit(_take)/gather | solution.py:77
  106.0 1.6 %fusion.20 = bf16[2048,128]{1,0:T(8,128)(2,1)S(1)} fusion(bf16[2048,128]{1,0:T(8,128)(2,1)S(1)} %copy-done.3, bf16[2048,128]{1,0:T(8,128)(2,1)S(1)} %gather_fusion.1, pred[2048]{0:T(1024)(128)(4,1)S(1)} %compare_and_fusion.3, pred[2048]{0:T(1024)(128)(4,1)S(1)} %get-tuple-element.10, pred[2048]{0:T(1024)(128)(4,1)S(1)} %get-tuple-element.12), kind=kLoop, calls=%fused_computation.37 | loop fusion | flops 786432 | bytes 1579008 | tf_op jit(solution)/shard_map/jit(_where)/select_n | solution.py:81
  107.6 0.8 copy-done.4
  108.8 4.0 %divide_convert_fusion = bf16[8,256,512]{2,1,0:T(8,128)(2,1)} fusion(bf16[8,256,128]{2,1,0:T(8,128)(2,1)S(1)} %convolution_convert_fusion.1, bf16[8,512,128]{2,1,0:T(8,128)(2,1)} %all-gather.2.cloned.1.call-done, bf16[128,128]{1,0:T(8,128)(2,1)S(1)} %copy-done.8), kind=kOutput, calls=%fused_computation.7 | convolution fusion | flops 408420352 | bytes 3702784 | tf_op jit(solution)/shard_map/rca,rha->rch/dot_general | solution.py:113
  112.8 2.5 %fusion.1 = bf16[8,256,128]{2,1,0:T(8,128)(2,1)S(1)} fusion(bf16[8,256,512]{2,1,0:T(8,128)(2,1)} %divide_convert_fusion, bf16[8,512,128]{2,1,0:T(8,128)(2,1)} %all-gather.2.cloned.1.call-done), kind=kOutput, calls=%fused_computation.13 | convolution fusion | flops 268959744 | bytes 3670016 | tf_op jit(solution)/shard_map/rch,rhe->rce/dot_general | solution.py:117
  115.4 8.1 %maximum_convert_fusion = bf16[2048,1024]{1,0:T(8,128)(2,1)} fusion(bf16[1,1024,1024]{2,1,0:T(8,128)(2,1)S(1)} %copy-done, bf16[256,1024]{1,0:T(8,128)(2,1)} %param.19, bf16[2048,128]{1,0:T(8,128)(2,1)S(1)} %bitcast.83, bf16[2048,128]{1,0:T(8,128)(2,1)S(1)} %copy-done.5), kind=kOutput, calls=%fused_computation.5 | convolution fusion | flops 5379194880 | bytes 7864320 | tf_op jit(solution)/shard_map/dot_general | solution.py:124
  123.5 3.4 %fusion.62 = f32[1,2048]{1,0:T(1,128)S(1)} fusion(bf16[2048,1024]{1,0:T(8,128)(2,1)} %maximum_convert_fusion, bf16[1024,1]{0,1:T(2,128)(2,1)S(1)} %reshape.312), kind=kOutput, calls=%fused_computation.132 | convolution fusion | flops 4194304 | bytes 4204544 | tf_op jit(solution)/shard_map/dot_general | solution.py:126
  (49 shorter events, 3.0 us)
Async XLA Ops:
  6.5 108.8 %copy-start = (bf16[1,1024,1024]{2,1,0:T(8,128)(2,1)S(1)}, bf16[1,1024,1024]{2,1,0:T(8,128)(2,1)}, u32[]{:S(2)}) copy-start(bf16[1,1024,1024]{2,1,0:T(8,128)(2,1)} %param.20) | copy-start | bytes 6291460
  6.5 25.2 %copy-start.1 = (f32[1024,128]{1,0:T(8,128)S(1)}, f32[1024,128]{1,0:T(8,128)}, u32[]{:S(2)}) copy-start(f32[1024,128]{1,0:T(8,128)} %param.14) | copy-start | bytes 1572868
  46.0 7.2 %copy-start.2 = (f32[2048,128]{1,0:T(8,128)S(1)}, f32[2048,128]{1,0:T(8,128)}, u32[]{:S(2)}) copy-start(f32[2048,128]{1,0:T(8,128)} %param.13) | copy-start | bytes 3145732
  48.6 27.6 %all-to-all-start.1 = ((bf16[16,256,128]{2,1,0:T(8,128)(2,1)}), bf16[16,256,128]{2,1,0:T(8,128)(2,1)}, u32[]{:S(2)}, u32[]{:S(2)}) async-start(bf16[16,256,128]{2,1,0:T(8,128)(2,1)} %select_convert_fusion), calls=%async_computation.1 | async-start | bytes 2097152 | tf_op jit(solution)/shard_map/all_to_all | solution.py:70
  53.0 55.8 %all-gather.2.cloned.1.call-start = ((), (), s32[]{:S(2)}) async-start(), calls=%async_computation.2 | async-start | bytes 1572864 | tf_op jit(solution)/shard_map/all_gather | solution.py:108
  87.4 11.7 %copy-start.7 = (bf16[1024]{0:T(1024)(128)(2,1)S(1)}, bf16[1024]{0:T(1024)(128)(2,1)}, u32[]{:S(2)}) copy-start(bf16[1024]{0:T(1024)(128)(2,1)} %param.21) | copy-start | bytes 6148
  99.0 6.9 %copy-start.3 = (bf16[2048,128]{1,0:T(8,128)(2,1)S(1)}, bf16[2048,128]{1,0:T(8,128)(2,1)}, u32[]{:S(2)}) copy-start(bf16[2048,128]{1,0:T(8,128)(2,1)} %gather_fusion.2) | copy-start | bytes 1572868
  99.0 9.4 %copy-start.6 = (bf16[128,128]{1,0:T(8,128)(2,1)S(1)}, bf16[128,128]{1,0:T(8,128)(2,1)}, u32[]{:S(2)}) copy-start(bf16[128,128]{1,0:T(8,128)(2,1)} %param.17) | copy-start | bytes 98308
  99.1 9.7 %copy-start.8 = (bf16[128,128]{1,0:T(8,128)(2,1)S(1)}, bf16[128,128]{1,0:T(8,128)(2,1)}, u32[]{:S(2)}) copy-start(bf16[128,128]{1,0:T(8,128)(2,1)} %param.18) | copy-start | bytes 98308
  107.6 0.8 copy-start.4
  108.7 6.7 %copy-start.5 = (bf16[2048,128]{1,0:T(8,128)(2,1)S(1)}, bf16[2048,128]{1,0:T(8,128)(2,1)}, u32[]{:S(2)}) copy-start(bf16[2048,128]{1,0:T(8,128)(2,1)} %copy-done.4) | copy-start | bytes 1572868
Sparse Core Ops, SparseCore 0:
  91.5 9.2 all-gather.1

commit v2 on v0

v2 whole, which is shorter than its diff:
```python
import math

import jax
import jax.numpy as jnp
from jax import lax
from jax.experimental import pallas as pl
from jax.experimental.pallas import tpu as pltpu
from jax.sharding import PartitionSpec as P

UNROLL = 32
GROUP = 2


def score_kernel(
    hist_ref,
    cand_ref,
    hot_ref,
    cold_ref,
    w_query_ref,
    w_key_ref,
    w_first_ref,
    w_second_ref,
    w_out_ref,
    out_ref,
    table,
    history,
    candidates,
):
    shards, requests, h_dev = hist_ref.shape
    c_dev = cand_ref.shape[1]
    hot_rows, width = hot_ref.shape
    h_total = shards * h_dev
    score_scale = 1.0 / math.sqrt(w_query_ref.shape[1])
    pool_scale = 1.0 / math.sqrt(h_total)

    table[pl.ds(0, hot_rows), :] = hot_ref[...]
    step = 512

    @pl.loop(0, cold_ref.shape[0] // step)
    def _(i):
        at = pl.multiple_of(i * step, step)
        to = pl.multiple_of(hot_rows + i * step, step)
        table[pl.ds(to, step), :] = cold_ref[pl.ds(at, step), :].astype(jnp.float32)

    @pl.loop(0, requests)
    def _(r):
        for s in range(shards):

            @pl.loop(0, h_dev // UNROLL)
            def _(block):
                base = pl.multiple_of(block * UNROLL, UNROLL)
                for u in range(UNROLL):
                    row = hist_ref[s, r, base + u]
                    history[r, pl.ds(s * h_dev + base + u, 1), :] = table[pl.ds(row, 1), :]

        @pl.loop(0, c_dev // UNROLL)
        def _(block):
            base = pl.multiple_of(block * UNROLL, UNROLL)
            for u in range(UNROLL):
                row = cand_ref[r, base + u]
                candidates[r, pl.ds(base + u, 1), :] = table[pl.ds(row, 1), :]

    w_out = jnp.broadcast_to(w_out_ref[...], (16, w_out_ref.shape[1]))

    @pl.loop(0, requests // GROUP)
    def _(g):
        joined = []
        for q in range(GROUP):
            r = g * GROUP + q
            hist = history[r].astype(jnp.bfloat16)
            cand = candidates[r].astype(jnp.bfloat16)
            query = jnp.dot(cand, w_query_ref[...], preferred_element_type=jnp.float32).astype(
                jnp.bfloat16
            )
            key = jnp.dot(hist, w_key_ref[...], preferred_element_type=jnp.float32).astype(
                jnp.bfloat16
            )
            logits = lax.dot_general(
                query, key, (((1,), (1,)), ((), ())), preferred_element_type=jnp.float32
            )
            attend = jax.nn.sigmoid(logits * score_scale).astype(jnp.bfloat16)
            pooled = jnp.dot(attend, hist, preferred_element_type=jnp.float32) * pool_scale
            joined.append(jnp.concatenate([cand, pooled.astype(jnp.bfloat16)], axis=1))
        joined = jnp.concatenate(joined, axis=0)
        first = jnp.dot(joined, w_first_ref[...], preferred_element_type=jnp.float32)
        first = jnp.maximum(first, 0.0).astype(jnp.bfloat16)
        deep = jnp.dot(first, w_second_ref[...], preferred_element_type=jnp.float32)
        deep = jnp.maximum(deep, 0.0).astype(jnp.bfloat16)
        ranked = lax.dot_general(
            w_out, deep, (((1,), (1,)), ((), ())), preferred_element_type=jnp.float32
        )
        for q in range(GROUP):
            out_ref[pl.ds(g * GROUP + q, 1), :] = ranked[0:1, q * c_dev : (q + 1) * c_dev]


def body(
    hot_item_table, cold_item_table, hist_rows, cand_rows, w_query, w_key, w_first, w_second, w_out
):
    requests, h_dev = hist_rows.shape
    c_dev = cand_rows.shape[1]
    hot_rows, width = hot_item_table.shape
    cold_all = lax.all_gather(cold_item_table.astype(jnp.bfloat16), "table", axis=0, tiled=True)
    hist_all = lax.all_gather(hist_rows, "score", axis=0)
    shards = hist_all.shape[0]
    vmem = pl.BlockSpec(memory_space=pltpu.VMEM)
    smem = pl.BlockSpec(memory_space=pltpu.SMEM)
    return pl.pallas_call(
        score_kernel,
        out_shape=jax.ShapeDtypeStruct((requests, c_dev), jnp.float32),
        in_specs=[smem, smem] + [vmem] * 7,
        out_specs=vmem,
        scratch_shapes=[
            pltpu.VMEM((hot_rows + cold_all.shape[0], width), jnp.float32),
            pltpu.VMEM((requests, shards * h_dev, width), jnp.float32),
            pltpu.VMEM((requests, c_dev, width), jnp.float32),
        ],
        compiler_params=pltpu.CompilerParams(vmem_limit_bytes=56 * 2**20),
        name="score_candidates",
    )(
        hist_all,
        cand_rows,
        hot_item_table,
        cold_all,
        w_query,
        w_key,
        w_first,
        w_second[0],
        w_out[None, :],
    )


def solution(mesh):
    return jax.shard_map(
        body,
        mesh=mesh,
        in_specs=(
            P(),
            P("table", None),
            P("table", "score"),
            P("table", "score"),
            P(),
            P(),
            P(),
            P(),
            P(),
        ),
        out_specs=P("table", "score"),
        check_vma=False,
    )
```

time: 135 us -> 127 us (0.941)
  waiting for transfers between devices: 15.4 us -> 76 us
  local copies, waits for them, and re-layouts: 50.3 us -> 1.27 us
  Pallas kernels: 0 us -> 31.1 us
  matrix products: 23 us -> 0 us
  blocking collectives: 15.4 us -> 3.38 us
  other arithmetic: 11.8 us -> 1.76 us
  starting transfers between devices: 4.55 us -> 0.01 us
    all_gather x1, waiting for transfers between devices: 0.02 us -> 76 us  [body(): lax.all_gather(cold_item_table.astype(jnp.bfloat16), 'table', axis=0, til...]
    gather x5 -> x0, local copies, waits for them, and re-layouts: 45.1 us -> none  [the longest x2 15.6 us: gather_owner_rows(): picked = jnp.take(flat_rows, jnp.where(is_cold, flat_index, 0), axis=0)]
    pallas_call x0 -> x1, Pallas kernels: none -> 31.1 us  [body(): pl.pallas_call(score_kernel, out_shape=jax.ShapeDtypeStruct((requests, c_...]
    dot_general x9 -> x0, matrix products: 23 us -> none  [the longest x1 8.13 us: body(): jnp.dot(hidden, w_second[0], preferred_element_type=jnp.float32)]
    all_to_all x1 -> x0, blocking collectives: 15.4 us -> none  [gather_owner_rows(): lax.all_to_all(wanted_all, 'table', split_axis=0, concat_axis=0, tiled=True)]
    all_to_all x1 -> x0, waiting for transfers between devices: 15.4 us -> none  [gather_owner_rows(): lax.all_to_all(cold_rows, 'table', split_axis=0, concat_axis=0, tiled=True)]
    select_n x5 -> x0, other arithmetic: 5.73 us -> none  [the longest x2 5.69 us: gather_owner_rows(): results.append(jnp.where(is_cold[:, None], picked, hot_rows))]
    all_to_all x1 -> x0, starting transfers between devices: 4.33 us -> none  [gather_owner_rows(): lax.all_to_all(cold_rows, 'table', split_axis=0, concat_axis=0, tiled=True)]
  transfers between devices with their start and end apart: 2 -> 1, of which waited for: 1 -> 1; matrix products, arithmetic and copies ran while one was open for 18% -> 1% of each run, Pallas kernels for 0% -> 0%
where the time goes in v2:
time: 127 us
  waiting for transfers between devices  76 us (60%)
  Pallas kernels  31.1 us (24%)
  between operations  13.4 us (11%)
  blocking collectives  3.38 us (3%)
  other arithmetic  1.76 us (1%)
  local copies, waits for them, and re-layouts  1.27 us (1%)
    all_gather x1, waiting for transfers between devices, body(): lax.all_gather(cold_item_table.astype(jnp.bfloat16), 'table', axis=0, til...  76 us
    pallas_call x1, Pallas kernels, body(): pl.pallas_call(score_kernel, out_shape=jax.ShapeDtypeStruct((requests, c_...  31.1 us
    all_gather x1, blocking collectives, body(): hist_all = lax.all_gather(hist_rows, 'score', axis=0)  3.38 us
  transfers between devices with their start and end apart: 1, of which 1 were waited for; matrix products, arithmetic and copies ran while one was open for 1% of the time, Pallas kernels for 0%

profile of v2, /device:TPU:0, one launch (start us, length us, event | category | flops | bytes accessed | tf_op | source)
XLA Modules:
  0.0 126.9 jit_solution(17079993976562446544)
XLA Ops:
  6.5 0.0 all-gather.3.cloned.1.call-start
  6.5 1.8 %convert_element_type.3 = bf16[1024,128]{1,0:T(8,128)(2,1)} convert(f32[1024,128]{1,0:T(8,128)} %param.10) | non-fusion elementwise | flops 131072 | bytes 786432 | tf_op jit(solution)/shard_map/convert_element_type | solution.py:102
  8.3 0.0 all-gather.3.cloned.1.call-update
  8.3 1.3 %broadcast_in_dim.3.w_out_ref = bf16[1,1024]{1,0:T(2,128)(2,1)} reshape(bf16[1024]{0:T(1024)(128)(2,1)} %param.17) | data formatting | bytes 4096 | tf_op jit(solution)/shard_map/broadcast_in_dim | solution.py:128
  9.6 3.4 %all-gather = s32[16,256]{1,0:T(8,128)} all-gather(s32[8,256]{1,0:T(8,128)} %param.11), channel_id=2, replica_groups=mesh['table'=16,'score'=2] {'score'}, dimensions={0}, use_global_device_ids=true | all-gather | bytes 24576 | tf_op jit(solution)/shard_map/all_gather | solution.py:103
  13.0 76.0 %all-gather.3.cloned.1.call-done.cold_ref = bf16[16384,128]{1,0:T(8,128)(2,1)} async-done(((bf16[1024,128]{1,0:T(8,128)(2,1)}), bf16[16384,128]{1,0:T(8,128)(2,1)}) %all-gather.3.cloned.1.call-update) | async-done | bytes 4194320 | tf_op jit(solution)/shard_map/all_gather | solution.py:102
  88.9 31.1 %score_candidates.1 = f32[8,256]{1,0:T(8,128)} custom-call(s32[2,8,256]{2,1,0:T(8,128)} %bitcast.3, s32[8,256]{1,0:T(8,128)} %cand_ref.1, f32[2048,128]{1,0:T(8,128)} %hot_ref.1, bf16[16384,128]{1,0:T(8,128)(2,1)} %all-gather.3.cloned.1.call-done.cold_ref, bf16[128,128]{1,0:T(8,128)(2,1)} %w_query_ref.1, bf16[128,128]{1,0:T(8,128)(2,1)} %w_key_ref.1, ...), custom_call_target="tpu_custom_call" | custom-call | tf_op jit(solution)/shard_map/score_candidates/pallas_call | solution.py:107
Async XLA Ops:
  6.5 82.4 %all-gather.3.cloned.1.call-start = ((), (), s32[]{:S(2)}) async-start(), calls=%async_computation | async-start | bytes 4456448 | tf_op jit(solution)/shard_map/all_gather | solution.py:102
Sparse Core Ops, SparseCore 0:
  10.1 78.7 all-gather.2

commit v3 on v2

--- a/solution.py
+++ b/solution.py
@@ -1,3 +1,4 @@
+import functools
 import math
 
 import jax
@@ -93,14 +94,279 @@
             out_ref[pl.ds(g * GROUP + q, 1), :] = ranked[0:1, q * c_dev : (q + 1) * c_dev]
 
 
+MESH = pl.DeviceIdType.MESH
+
+
+def spread_kernel(
+    n_table,
+    n_score,
+    cold_ref,
+    hist_ref,
+    out_ref,
+    hist_out,
+    own,
+    recv_main,
+    recv_diag,
+    recv_peer,
+    send_up,
+    send_down,
+    send_x,
+    send_y,
+    send_half_x,
+    send_half_y,
+    send_peer,
+    hist_send,
+    hist_recv,
+    local_sem,
+):
+    depth = n_table // 4
+    me = lax.axis_index("table")
+    c = lax.axis_index("score")
+    z, y, x = me // 4, (me // 2) % 2, me % 2
+    rows = own.shape[1]
+    half = rows // 2
+
+    def at(zz, yy, xx):
+        return (zz * 2 + yy) * 2 + xx
+
+    def device(owner):
+        return {"table": owner, "score": c}
+
+    to_x, to_y = device(at(z, y, 1 - x)), device(at(z, 1 - y, x))
+    to_up, to_down = device(at(z + 1, y, x)), device(at(z - 1, y, x))
+    has_up, has_down = z < depth - 1, z > 0
+    peers = [{"table": me, "score": (c + k) % n_score} for k in range(1, n_score)]
+
+    barrier = pltpu.get_barrier_semaphore()
+    for target in [to_x, to_y] + peers:
+        pl.semaphore_signal(barrier, inc=1, device_id=target, device_id_type=MESH)
+    for cond, target in ((has_up, to_up), (has_down, to_down)):
+
+        @pl.when(cond)
+        def _():
+            pl.semaphore_signal(barrier, inc=1, device_id=target, device_id_type=MESH)
+
+    for s in range(n_score):
+        own[s] = cold_ref[pl.ds(s * rows, rows), :].astype(jnp.bfloat16)
+
+    along_z = has_up.astype(jnp.int32) + has_down.astype(jnp.int32)
+    pl.semaphore_wait(barrier, 2 + len(peers) + along_z)
+
+    def copy(src, dst, send, recv, target):
+        return pltpu.make_async_remote_copy(
+            src_ref=src,
+            dst_ref=dst,
+            send_sem=send,
+            recv_sem=recv,
+            device_id=target,
+            device_id_type=MESH,
+        )
+
+    def whole(owner, send, target, src=None):
+        src = out_ref.at[owner, c] if src is None else src
+        return copy(src, out_ref.at[owner, c], send, recv_main.at[owner], target)
+
+    def part(owner, zz, which, send, target):
+        block = out_ref.at[owner, c, pl.ds(which * half, half)]
+        return copy(block, block, send, recv_diag.at[zz, which], target)
+
+    def to_peers(owner):
+        return [
+            copy(
+                out_ref.at[owner, c],
+                out_ref.at[owner, c],
+                send_peer.at[owner, k],
+                recv_peer.at[owner, c],
+                target,
+            )
+            for k, target in enumerate(peers)
+        ]
+
+    def start(copies):
+        for one in copies:
+            one.start()
+
+    def column(zz, src=None):
+        owner = at(zz, y, x)
+        return [whole(owner, send_x.at[zz], to_x, src), whole(owner, send_y.at[zz], to_y, src)]
+
+    def upward(zz, src=None):
+        return whole(at(zz, y, x), send_up.at[zz], to_up, src)
+
+    def downward(zz, src=None):
+        return whole(at(zz, y, x), send_down.at[zz], to_down, src)
+
+    mine = own.at[c]
+
+    @pl.when(has_up)
+    def _():
+        upward(z, mine).start()
+
+    @pl.when(has_down)
+    def _():
+        downward(z, mine).start()
+
+    start(column(z, mine))
+    hist_copies = [
+        copy(hist_ref, hist_out.at[c], hist_send.at[k], hist_recv.at[c], target)
+        for k, target in enumerate(peers)
+    ]
+    start(hist_copies)
+    local = [
+        pltpu.make_async_copy(own, out_ref.at[me], local_sem.at[0]),
+        pltpu.make_async_copy(hist_ref, hist_out.at[c], local_sem.at[1]),
+    ]
+    start(local)
+
+    def sides(d):
+        if d == 0:
+            return [(z, None)]
+        return [(z - d, z - d >= 0), (z + d, z + d < depth)]
+
+    def guarded(cond, run):
+        if cond is None:
+            run()
+        else:
+            pl.when(cond)(run)
+
+    def from_column(d):
+        for zz, cond in sides(d):
+
+            def run(zz=zz):
+                owner = at(zz, y, x)
+                whole(owner, send_x.at[zz], to_x).wait_recv()
+
+                @pl.when(jnp.logical_and(zz < z, has_up))
+                def _():
+                    upward(zz).start()
+
+                @pl.when(jnp.logical_and(zz > z, has_down))
+                def _():
+                    downward(zz).start()
+
+                start(column(zz))
+                start(to_peers(owner))
+
+            guarded(cond, run)
+
+    def from_sides(d):
+        for zz, cond in sides(d):
+
+            def run(zz=zz):
+                owner = at(zz, y, 1 - x)
+                whole(owner, send_x.at[zz], to_x).wait_recv()
+                part(owner, zz, 0, send_half_y.at[zz], to_y).start()
+                start(to_peers(owner))
+                owner = at(zz, 1 - y, x)
+                whole(owner, send_x.at[zz], to_x).wait_recv()
+                part(owner, zz, 1, send_half_x.at[zz], to_x).start()
+                start(to_peers(owner))
+
+            guarded(cond, run)
+
+    def from_diagonal(d):
+        for zz, cond in sides(d):
+
+            def run(zz=zz):
+                owner = at(zz, 1 - y, 1 - x)
+                part(owner, zz, 0, send_half_y.at[zz], to_y).wait_recv()
+                part(owner, zz, 1, send_half_x.at[zz], to_x).wait_recv()
+                start(to_peers(owner))
+
+            guarded(cond, run)
+
+    for d in range(1, depth + 2):
+        if d < depth:
+            from_column(d)
+        if d - 1 < depth:
+            from_sides(d - 1)
+        if 0 <= d - 2:
+            from_diagonal(d - 2)
+
+    def finish(zz, src=None):
+        for one in column(zz, src):
+            one.wait_send()
+        part(at(zz, y, 1 - x), zz, 0, send_half_y.at[zz], to_y).wait_send()
+        part(at(zz, 1 - y, x), zz, 1, send_half_x.at[zz], to_x).wait_send()
+
+        @pl.when(jnp.logical_and(zz <= z, has_up))
+        def _():
+            upward(zz, src).wait_send()
+
+        @pl.when(jnp.logical_and(zz >= z, has_down))
+        def _():
+            downward(zz, src).wait_send()
+
+    for one in hist_copies:
+        one.wait_send()
+    for one in local:
+        one.wait()
+    for k in range(1, n_score):
+        other = (c + k) % n_score
+        copy(hist_ref, hist_out.at[other], hist_send.at[0], hist_recv.at[other], to_x).wait_recv()
+    for zz in range(depth):
+        finish(zz)
+        for yy in range(2):
+            for xx in range(2):
+                owner = at(zz, yy, xx)
+
+                @pl.when(owner != me)
+                def _():
+                    for one in to_peers(owner):
+                        one.wait_send()
+                    for k in range(1, n_score):
+                        other = (c + k) % n_score
+                        block = out_ref.at[owner, other]
+                        copy(
+                            block, block, send_peer.at[0, 0], recv_peer.at[owner, other], to_x
+                        ).wait_recv()
+
+
+def spread(cold_item_table, hist_rows):
+    n_table, n_score = lax.axis_size("table"), lax.axis_size("score")
+    cold_rows, width = cold_item_table.shape
+    depth, rows = n_table // 4, cold_rows // n_score
+    dma = pltpu.SemaphoreType.DMA
+    anywhere = pl.BlockSpec(memory_space=pl.ANY)
+    cold_all, hist_all = pl.pallas_call(
+        functools.partial(spread_kernel, n_table, n_score),
+        out_shape=(
+            jax.ShapeDtypeStruct((n_table, n_score, rows, width), jnp.bfloat16),
+            jax.ShapeDtypeStruct((n_score,) + hist_rows.shape, jnp.int32),
+        ),
+        in_specs=[pl.BlockSpec(memory_space=pltpu.VMEM)] * 2,
+        out_specs=(anywhere, anywhere),
+        scratch_shapes=[
+            pltpu.VMEM((n_score, rows, width), jnp.bfloat16),
+            dma((n_table,)),
+            dma((depth, 2)),
+            dma((n_table, n_score)),
+            dma((depth,)),
+            dma((depth,)),
+            dma((depth,)),
+            dma((depth,)),
+            dma((depth,)),
+            dma((depth,)),
+            dma((n_table, n_score - 1)),
+            dma((n_score - 1,)),
+            dma((n_score,)),
+            dma((2,)),
+        ],
+        compiler_params=pltpu.CompilerParams(
+            collective_id=0, has_side_effects=True, vmem_limit_bytes=8 * 2**20
+        ),
+        name="spread_cold_rows",
+    )(cold_item_table, hist_rows)
+    return cold_all.reshape(n_table * cold_rows, width), hist_all
+
+
 def body(
     hot_item_table, cold_item_table, hist_rows, cand_rows, w_query, w_key, w_first, w_second, w_out
 ):
     requests, h_dev = hist_rows.shape
     c_dev = cand_rows.shape[1]
     hot_rows, width = hot_item_table.shape
-    cold_all = lax.all_gather(cold_item_table.astype(jnp.bfloat16), "table", axis=0, tiled=True)
-    hist_all = lax.all_gather(hist_rows, "score", axis=0)
+    cold_all, hist_all = spread(cold_item_table, hist_rows)
     shards = hist_all.shape[0]
     vmem = pl.BlockSpec(memory_space=pltpu.VMEM)
     smem = pl.BlockSpec(memory_space=pltpu.SMEM)

time: 127 us -> 64.3 us (0.51)
  waiting for transfers between devices: 76 us -> 0 us
  Pallas kernels: 31.1 us -> 58.5 us
  between operations: 13.4 us -> 0.02 us
  local copies, waits for them, and re-layouts: 1.27 us -> 5.54 us
  blocking collectives: 3.38 us -> 0 us
  other arithmetic: 1.76 us -> 0 us
    all_gather x1 -> x0, waiting for transfers between devices: 76 us -> none  [body(): lax.all_gather(cold_item_table.astype(jnp.bfloat16), 'table', axis=0, til...]
    pallas_call x0 -> x1, Pallas kernels: none -> 27.4 us  [spread(): pl.pallas_call(functools.partial(spread_kernel, n_table, n_score), out_sh...]
    unnamed x0 -> x8, local copies, waits for them, and re-layouts: none -> 4.26 us
    all_gather x1 -> x0, blocking collectives: 3.38 us -> none  [body(): hist_all = lax.all_gather(hist_rows, 'score', axis=0)]
    convert_element_type x1 -> x0, other arithmetic: 1.76 us -> none  [body(): cold_item_table.astype(jnp.bfloat16)]
  transfers between devices with their start and end apart: 1 -> 0, of which waited for: 1 -> 0; matrix products, arithmetic and copies ran while one was open for 1% -> 0% of each run, Pallas kernels for 0% -> 0%
where the time goes in v3:
time: 64.3 us; the launch traced here: 64 us
  Pallas kernels  58.5 us (91%)
  local copies, waits for them, and re-layouts  5.54 us (9%)
    pallas_call x1, Pallas kernels, body(): pl.pallas_call(score_kernel, out_shape=jax.ShapeDtypeStruct((requests, c_...  31.1 us
    pallas_call x1, Pallas kernels, spread(): pl.pallas_call(functools.partial(spread_kernel, n_table, n_score), out_sh...  27.4 us
    unnamed x8, local copies, waits for them, and re-layouts  4.26 us

profile of v3, /device:TPU:0, one launch (start us, length us, event | category | flops | bytes accessed | tf_op | source)
XLA Modules:
  0.0 64.0 jit_solution(8228522974389305254)
XLA Ops:
  0.0 1.3 %broadcast_in_dim.3.w_out_ref = bf16[1,1024]{1,0:T(2,128)(2,1)} reshape(bf16[1024]{0:T(1024)(128)(2,1)} %param.17) | data formatting | bytes 4096 | tf_op jit(solution)/shard_map/broadcast_in_dim | solution.py:394
  1.3 0.0 copy-start.1
  1.3 1.0 %copy-done.1 = f32[1024,128]{1,0:T(8,128)S(1)} copy-done((f32[1024,128]{1,0:T(8,128)S(1)}, f32[1024,128]{1,0:T(8,128)}, u32[]{:S(2)}) %copy-start.1) | copy-done | bytes 524312
  2.3 0.0 copy-start.3
  2.3 0.7 %copy-done.3 = s32[8,256]{1,0:T(8,128)S(1)} copy-done((s32[8,256]{1,0:T(8,128)S(1)}, s32[8,256]{1,0:T(8,128)}, u32[]{:S(2)}) %copy-start.3) | copy-done | bytes 8216
  3.0 27.4 %spread_cold_rows.1 = (bf16[16,2,512,128]{3,2,1,0:T(8,128)(2,1)S(1)}, s32[2,8,256]{2,1,0:T(8,128)S(1)}) custom-call(f32[1024,128]{1,0:T(8,128)S(1)} %copy-done.1, s32[8,256]{1,0:T(8,128)S(1)} %copy-done.3), custom_call_target="tpu_custom_call" | custom-call | tf_op jit(solution)/shard_map/spread_cold_rows/pallas_call | solution.py:331
  30.4 0.0 copy-start
  30.4 1.9 %copy-done = bf16[16,2,512,128]{3,2,1,0:T(8,128)(2,1)} copy-done((bf16[16,2,512,128]{3,2,1,0:T(8,128)(2,1)}, bf16[16,2,512,128]{3,2,1,0:T(8,128)(2,1)S(1)}, u32[]{:S(2)}) %copy-start) | copy-done | bytes 4194328
  32.4 0.0 copy-start.2
  32.4 0.6 copy-done.2
  33.0 31.1 %score_candidates.1 = f32[8,256]{1,0:T(8,128)} custom-call(s32[2,8,256]{2,1,0:T(8,128)} %copy-done.2, s32[8,256]{1,0:T(8,128)} %cand_ref.1, f32[2048,128]{1,0:T(8,128)} %hot_ref.1, bf16[16384,128]{1,0:T(8,128)(2,1)} %bitcast.2, bf16[128,128]{1,0:T(8,128)(2,1)} %w_query_ref.1, bf16[128,128]{1,0:T(8,128)(2,1)} %w_key_ref.1, bf16[256,1024]{1,0:T(8,128)(2,1)} %w_first_ref.1, ...), custom_call_target="tpu_custom_call" | custom-call | tf_op jit(solution)/shard_map/score_candidates/pallas_call | solution.py:373
Async XLA Ops:
  1.3 1.0 %copy-start.1 = (f32[1024,128]{1,0:T(8,128)S(1)}, f32[1024,128]{1,0:T(8,128)}, u32[]{:S(2)}) copy-start(f32[1024,128]{1,0:T(8,128)} %cold_ref.1) | copy-start | bytes 1572868
  2.3 0.7 %copy-start.3 = (s32[8,256]{1,0:T(8,128)S(1)}, s32[8,256]{1,0:T(8,128)}, u32[]{:S(2)}) copy-start(s32[8,256]{1,0:T(8,128)} %hist_ref.1) | copy-start | bytes 24580
  30.4 1.9 %copy-start = (bf16[16,2,512,128]{3,2,1,0:T(8,128)(2,1)}, bf16[16,2,512,128]{3,2,1,0:T(8,128)(2,1)S(1)}, u32[]{:S(2)}) copy-start(bf16[16,2,512,128]{3,2,1,0:T(8,128)(2,1)S(1)} %get-tuple-element.8) | copy-start | bytes 12582916
  32.4 0.6 copy-start.2

commit v4 on v3

--- a/solution.py
+++ b/solution.py
@@ -46,22 +46,18 @@
     @pl.loop(0, requests)
     def _(r):
         for s in range(shards):
-
-            @pl.loop(0, h_dev // UNROLL)
-            def _(block):
-                base = pl.multiple_of(block * UNROLL, UNROLL)
+            for start in range(0, h_dev, UNROLL):
+                rows = [hist_ref[s, r, start + u] for u in range(UNROLL)]
+                got = [table[pl.ds(row, 1), :] for row in rows]
                 for u in range(UNROLL):
-                    row = hist_ref[s, r, base + u]
-                    history[r, pl.ds(s * h_dev + base + u, 1), :] = table[pl.ds(row, 1), :]
-
-        @pl.loop(0, c_dev // UNROLL)
-        def _(block):
-            base = pl.multiple_of(block * UNROLL, UNROLL)
+                    history[r, pl.ds(s * h_dev + start + u, 1), :] = got[u]
+        for start in range(0, c_dev, UNROLL):
+            rows = [cand_ref[r, start + u] for u in range(UNROLL)]
+            got = [table[pl.ds(row, 1), :] for row in rows]
             for u in range(UNROLL):
-                row = cand_ref[r, base + u]
-                candidates[r, pl.ds(base + u, 1), :] = table[pl.ds(row, 1), :]
-
-    w_out = jnp.broadcast_to(w_out_ref[...], (16, w_out_ref.shape[1]))
+                candidates[r, pl.ds(start + u, 1), :] = got[u]
+
+    w_out = jnp.broadcast_to(w_out_ref[...][None, :], (16, w_out_ref.shape[0]))
 
     @pl.loop(0, requests // GROUP)
     def _(g):
@@ -79,7 +75,7 @@
             logits = lax.dot_general(
                 query, key, (((1,), (1,)), ((), ())), preferred_element_type=jnp.float32
             )
-            attend = jax.nn.sigmoid(logits * score_scale).astype(jnp.bfloat16)
+            attend = (jnp.tanh(logits * (0.5 * score_scale)) * 0.5 + 0.5).astype(jnp.bfloat16)
             pooled = jnp.dot(attend, hist, preferred_element_type=jnp.float32) * pool_scale
             joined.append(jnp.concatenate([cand, pooled.astype(jnp.bfloat16)], axis=1))
         joined = jnp.concatenate(joined, axis=0)
@@ -391,7 +387,7 @@
         w_key,
         w_first,
         w_second[0],
-        w_out[None, :],
+        w_out,
     )
 
 

time: 64.3 us -> 53.4 us (0.83)
  Pallas kernels: 58.5 us -> 49 us
  local copies, waits for them, and re-layouts: 5.54 us -> 4.26 us
    pallas_call x1, Pallas kernels: 31.1 us -> 21.6 us  [body(): pl.pallas_call(score_kernel, out_shape=jax.ShapeDtypeStruct((requests, c_...]
    broadcast_in_dim x1 -> x0, local copies, waits for them, and re-layouts: 1.27 us -> none  [body(): w_out[None, :]]
where the time goes in v4:
time: 53.4 us; the launch traced here: 53.2 us
  Pallas kernels  49 us (92%)
  local copies, waits for them, and re-layouts  4.26 us (8%)
    pallas_call x1, Pallas kernels, spread(): pl.pallas_call(functools.partial(spread_kernel, n_table, n_score), out_sh...  27.4 us
    pallas_call x1, Pallas kernels, body(): pl.pallas_call(score_kernel, out_shape=jax.ShapeDtypeStruct((requests, c_...  21.6 us
    unnamed x8, local copies, waits for them, and re-layouts  4.26 us

profile of v4, /device:TPU:0, one launch (start us, length us, event | category | flops | bytes accessed | tf_op | source)
XLA Modules:
  0.0 53.2 jit_solution(2739634217573748577)
XLA Ops:
  0.0 0.0 copy-start.1
  0.0 1.0 %copy-done.1 = f32[1024,128]{1,0:T(8,128)S(1)} copy-done((f32[1024,128]{1,0:T(8,128)S(1)}, f32[1024,128]{1,0:T(8,128)}, u32[]{:S(2)}) %copy-start.1) | copy-done | bytes 524312
  1.0 0.0 copy-start.3
  1.0 0.7 %copy-done.3 = s32[8,256]{1,0:T(8,128)S(1)} copy-done((s32[8,256]{1,0:T(8,128)S(1)}, s32[8,256]{1,0:T(8,128)}, u32[]{:S(2)}) %copy-start.3) | copy-done | bytes 8216
  1.7 27.4 %spread_cold_rows.1 = (bf16[16,2,512,128]{3,2,1,0:T(8,128)(2,1)S(1)}, s32[2,8,256]{2,1,0:T(8,128)S(1)}) custom-call(f32[1024,128]{1,0:T(8,128)S(1)} %copy-done.1, s32[8,256]{1,0:T(8,128)S(1)} %copy-done.3), custom_call_target="tpu_custom_call" | custom-call | tf_op jit(solution)/shard_map/spread_cold_rows/pallas_call | solution.py:327
  29.2 0.0 copy-start
  29.2 1.9 %copy-done = bf16[16,2,512,128]{3,2,1,0:T(8,128)(2,1)} copy-done((bf16[16,2,512,128]{3,2,1,0:T(8,128)(2,1)}, bf16[16,2,512,128]{3,2,1,0:T(8,128)(2,1)S(1)}, u32[]{:S(2)}) %copy-start) | copy-done | bytes 4194328
  31.1 0.0 copy-start.2
  31.1 0.6 %copy-done.2 = s32[2,8,256]{2,1,0:T(8,128)} copy-done((s32[2,8,256]{2,1,0:T(8,128)}, s32[2,8,256]{2,1,0:T(8,128)S(1)}, u32[]{:S(2)}) %copy-start.2) | copy-done | bytes 16408
  31.7 21.6 %score_candidates.1 = f32[8,256]{1,0:T(8,128)} custom-call(s32[2,8,256]{2,1,0:T(8,128)} %copy-done.2, s32[8,256]{1,0:T(8,128)} %cand_ref.1, f32[2048,128]{1,0:T(8,128)} %hot_ref.1, bf16[16384,128]{1,0:T(8,128)(2,1)} %bitcast.2, bf16[128,128]{1,0:T(8,128)(2,1)} %w_query_ref.1, bf16[128,128]{1,0:T(8,128)(2,1)} %w_key_ref.1, bf16[256,1024]{1,0:T(8,128)(2,1)} %w_first_ref.1, ...), custom_call_target="tpu_custom_call" | custom-call | tf_op jit(solution)/shard_map/score_candidates/pallas_call | solution.py:369
Async XLA Ops:
  0.0 1.0 %copy-start.1 = (f32[1024,128]{1,0:T(8,128)S(1)}, f32[1024,128]{1,0:T(8,128)}, u32[]{:S(2)}) copy-start(f32[1024,128]{1,0:T(8,128)} %cold_ref.1) | copy-start | bytes 1572868
  1.0 0.7 %copy-start.3 = (s32[8,256]{1,0:T(8,128)S(1)}, s32[8,256]{1,0:T(8,128)}, u32[]{:S(2)}) copy-start(s32[8,256]{1,0:T(8,128)} %hist_ref.1) | copy-start | bytes 24580
  29.2 1.9 %copy-start = (bf16[16,2,512,128]{3,2,1,0:T(8,128)(2,1)}, bf16[16,2,512,128]{3,2,1,0:T(8,128)(2,1)S(1)}, u32[]{:S(2)}) copy-start(bf16[16,2,512,128]{3,2,1,0:T(8,128)(2,1)S(1)} %get-tuple-element.8) | copy-start | bytes 12582916
  31.1 0.6 %copy-start.2 = (s32[2,8,256]{2,1,0:T(8,128)}, s32[2,8,256]{2,1,0:T(8,128)S(1)}, u32[]{:S(2)}) copy-start(s32[2,8,256]{2,1,0:T(8,128)S(1)} %get-tuple-element.7.hist_ref) | copy-start | bytes 49156

commit v5 on v4

--- a/solution.py
+++ b/solution.py
@@ -331,7 +331,7 @@
             jax.ShapeDtypeStruct((n_score,) + hist_rows.shape, jnp.int32),
         ),
         in_specs=[pl.BlockSpec(memory_space=pltpu.VMEM)] * 2,
-        out_specs=(anywhere, anywhere),
+        out_specs=(pl.BlockSpec(memory_space=pltpu.VMEM), anywhere),
         scratch_shapes=[
             pltpu.VMEM((n_score, rows, width), jnp.bfloat16),
             dma((n_table,)),
@@ -349,7 +349,7 @@
             dma((2,)),
         ],
         compiler_params=pltpu.CompilerParams(
-            collective_id=0, has_side_effects=True, vmem_limit_bytes=8 * 2**20
+            collective_id=0, has_side_effects=True, vmem_limit_bytes=4 * 2**20
         ),
         name="spread_cold_rows",
     )(cold_item_table, hist_rows)
@@ -376,7 +376,7 @@
             pltpu.VMEM((requests, shards * h_dev, width), jnp.float32),
             pltpu.VMEM((requests, c_dev, width), jnp.float32),
         ],
-        compiler_params=pltpu.CompilerParams(vmem_limit_bytes=56 * 2**20),
+        compiler_params=pltpu.CompilerParams(vmem_limit_bytes=36 * 2**20),
         name="score_candidates",
     )(
         hist_all,

time: 53.4 us -> 55.8 us (1.045)
  local copies, waits for them, and re-layouts: 4.26 us -> 8.48 us
  Pallas kernels: 49 us -> 46.7 us
    unnamed x8 -> x18, local copies, waits for them, and re-layouts: 4.26 us -> 8.48 us
    pallas_call x1, Pallas kernels: 21.6 us -> 19.3 us  [body(): pl.pallas_call(score_kernel, out_shape=jax.ShapeDtypeStruct((requests, c_...]
where the time goes in v5:
time: 55.8 us; the launch traced here: 55.2 us
  Pallas kernels  46.7 us (84%)
  local copies, waits for them, and re-layouts  8.48 us (15%)
    pallas_call x1, Pallas kernels, spread(): pl.pallas_call(functools.partial(spread_kernel, n_table, n_score), out_sh...  27.4 us
    pallas_call x1, Pallas kernels, body(): pl.pallas_call(score_kernel, out_shape=jax.ShapeDtypeStruct((requests, c_...  19.3 us
    unnamed x18, local copies, waits for them, and re-layouts  8.48 us

profile of v5, /device:TPU:0, one launch (start us, length us, event | category | flops | bytes accessed | tf_op | source)
XLA Modules:
  0.0 55.2 jit_solution(7454601724956443765)
XLA Ops:
  0.0 0.0 copy-start.3
  0.0 1.0 %copy-done.3 = f32[1024,128]{1,0:T(8,128)S(1)} copy-done((f32[1024,128]{1,0:T(8,128)S(1)}, f32[1024,128]{1,0:T(8,128)}, u32[]{:S(2)}) %copy-start.3) | copy-done | bytes 524312
  1.0 0.0 copy-start.6
  1.0 0.7 %copy-done.6 = s32[8,256]{1,0:T(8,128)S(1)} copy-done((s32[8,256]{1,0:T(8,128)S(1)}, s32[8,256]{1,0:T(8,128)}, u32[]{:S(2)}) %copy-start.6) | copy-done | bytes 8216
  1.7 27.4 %spread_cold_rows.1 = (bf16[16,2,512,128]{3,2,1,0:T(8,128)(2,1)S(1)}, s32[2,8,256]{2,1,0:T(8,128)S(1)}) custom-call(f32[1024,128]{1,0:T(8,128)S(1)} %copy-done.3, s32[8,256]{1,0:T(8,128)S(1)} %copy-done.6), custom_call_target="tpu_custom_call" | custom-call | tf_op jit(solution)/shard_map/spread_cold_rows/pallas_call | solution.py:327
  29.2 0.0 copy-start
  29.2 1.6 %copy-done = bf16[1,1024,1024]{2,1,0:T(8,128)(2,1)S(1)} copy-done((bf16[1,1024,1024]{2,1,0:T(8,128)(2,1)S(1)}, bf16[1,1024,1024]{2,1,0:T(8,128)(2,1)}, u32[]{:S(2)}) %copy-start) | copy-done | bytes 2097176
  30.7 0.0 copy-start.1
  30.8 1.2 %copy-done.1 = f32[2048,128]{1,0:T(8,128)S(1)} copy-done((f32[2048,128]{1,0:T(8,128)S(1)}, f32[2048,128]{1,0:T(8,128)}, u32[]{:S(2)}) %copy-start.1) | copy-done | bytes 1048600
  32.0 0.0 copy-start.2
  32.0 1.0 %copy-done.2 = bf16[256,1024]{1,0:T(8,128)(2,1)S(1)} copy-done((bf16[256,1024]{1,0:T(8,128)(2,1)S(1)}, bf16[256,1024]{1,0:T(8,128)(2,1)}, u32[]{:S(2)}) %copy-start.2) | copy-done | bytes 524312
  33.0 0.0 copy-start.4
  33.0 0.8 %copy-done.4 = bf16[128,128]{1,0:T(8,128)(2,1)S(1)} copy-done((bf16[128,128]{1,0:T(8,128)(2,1)S(1)}, bf16[128,128]{1,0:T(8,128)(2,1)}, u32[]{:S(2)}) %copy-start.4) | copy-done | bytes 32792
  33.8 0.0 copy-start.5
  33.8 0.8 %copy-done.5 = bf16[128,128]{1,0:T(8,128)(2,1)S(1)} copy-done((bf16[128,128]{1,0:T(8,128)(2,1)S(1)}, bf16[128,128]{1,0:T(8,128)(2,1)}, u32[]{:S(2)}) %copy-start.5) | copy-done | bytes 32792
  34.5 0.0 copy-start.7
  34.5 0.7 %copy-done.7 = s32[8,256]{1,0:T(8,128)S(1)} copy-done((s32[8,256]{1,0:T(8,128)S(1)}, s32[8,256]{1,0:T(8,128)}, u32[]{:S(2)}) %copy-start.7) | copy-done | bytes 8216
  35.2 0.0 copy-start.8
  35.2 0.7 %copy-done.8 = bf16[1024]{0:T(1024)(128)(2,1)S(1)} copy-done((bf16[1024]{0:T(1024)(128)(2,1)S(1)}, bf16[1024]{0:T(1024)(128)(2,1)}, u32[]{:S(2)}) %copy-start.8) | copy-done | bytes 2072
  35.9 19.3 %score_candidates.1 = f32[8,256]{1,0:T(8,128)} custom-call(s32[2,8,256]{2,1,0:T(8,128)S(1)} %get-tuple-element.7.hist_ref, s32[8,256]{1,0:T(8,128)S(1)} %copy-done.7, f32[2048,128]{1,0:T(8,128)S(1)} %copy-done.1, bf16[16384,128]{1,0:T(8,128)(2,1)S(1)} %bitcast.2, bf16[128,128]{1,0:T(8,128)(2,1)S(1)} %copy-done.4, bf16[128,128]{1,0:T(8,128)(2,1)S(1)} %copy-done.5, ...), custom_call_target="tpu_custom_call" | custom-call | tf_op jit(solution)/shard_map/score_candidates/pallas_call | solution.py:369
Async XLA Ops:
  0.0 1.0 %copy-start.3 = (f32[1024,128]{1,0:T(8,128)S(1)}, f32[1024,128]{1,0:T(8,128)}, u32[]{:S(2)}) copy-start(f32[1024,128]{1,0:T(8,128)} %cold_ref.1) | copy-start | bytes 1572868
  1.0 0.7 %copy-start.6 = (s32[8,256]{1,0:T(8,128)S(1)}, s32[8,256]{1,0:T(8,128)}, u32[]{:S(2)}) copy-start(s32[8,256]{1,0:T(8,128)} %hist_ref.1) | copy-start | bytes 24580
  29.2 1.6 %copy-start = (bf16[1,1024,1024]{2,1,0:T(8,128)(2,1)S(1)}, bf16[1,1024,1024]{2,1,0:T(8,128)(2,1)}, u32[]{:S(2)}) copy-start(bf16[1,1024,1024]{2,1,0:T(8,128)(2,1)} %param.16) | copy-start | bytes 6291460
  30.7 1.2 %copy-start.1 = (f32[2048,128]{1,0:T(8,128)S(1)}, f32[2048,128]{1,0:T(8,128)}, u32[]{:S(2)}) copy-start(f32[2048,128]{1,0:T(8,128)} %hot_ref.1) | copy-start | bytes 3145732
  32.0 1.0 %copy-start.2 = (bf16[256,1024]{1,0:T(8,128)(2,1)S(1)}, bf16[256,1024]{1,0:T(8,128)(2,1)}, u32[]{:S(2)}) copy-start(bf16[256,1024]{1,0:T(8,128)(2,1)} %w_first_ref.1) | copy-start | bytes 1572868
  33.0 0.8 %copy-start.4 = (bf16[128,128]{1,0:T(8,128)(2,1)S(1)}, bf16[128,128]{1,0:T(8,128)(2,1)}, u32[]{:S(2)}) copy-start(bf16[128,128]{1,0:T(8,128)(2,1)} %w_query_ref.1) | copy-start | bytes 98308
  33.8 0.8 %copy-start.5 = (bf16[128,128]{1,0:T(8,128)(2,1)S(1)}, bf16[128,128]{1,0:T(8,128)(2,1)}, u32[]{:S(2)}) copy-start(bf16[128,128]{1,0:T(8,128)(2,1)} %w_key_ref.1) | copy-start | bytes 98308
  34.5 0.7 %copy-start.7 = (s32[8,256]{1,0:T(8,128)S(1)}, s32[8,256]{1,0:T(8,128)}, u32[]{:S(2)}) copy-start(s32[8,256]{1,0:T(8,128)} %cand_ref.1) | copy-start | bytes 24580
  35.2 0.7 %copy-start.8 = (bf16[1024]{0:T(1024)(128)(2,1)S(1)}, bf16[1024]{0:T(1024)(128)(2,1)}, u32[]{:S(2)}) copy-start(bf16[1024]{0:T(1024)(128)(2,1)} %w_out_ref.1) | copy-start | bytes 6148
